TPU v7x, 32 devices: a whole 2x2x4 slice. The times are simulated.
32 devices in a mesh: groups: 2 (over y), wide: 8 (over z, x), narrow: 2 (over core).
Axes of the slice: x: 2, y: 2, z: 4, core: 2. Of those that a mesh axis runs over, the one named last changes fastest.
Arguments:
- tokens: bfloat16 [4096, 8192], P(('groups', 'wide'), 'narrow'), parts along dimension 0, may hold values from -6 to 6
- output_gradient: bfloat16 [4096, 1024], P(('groups', 'wide'), 'narrow'), parts along dimension 0, may hold values from -0.59765625 to 0.59765625
- value_weight: bfloat16 [8192, 1024], P('narrow', 'wide'), may hold values from -0.0625 to 0.0625
- adapter_down: bfloat16 [32, 8192, 64], P(('groups', 'wide'), 'narrow'), parts along dimension 0, may hold values from -0.0625 to 0.0625
- adapter_up: bfloat16 [32, 64, 1024], P(('groups', 'wide'), None, 'narrow'), parts along dimension 0, may hold values from -0.1875 to 0.1875
- counts: int32 [16, 16], P(('groups', 'wide')), parts along dimension 0, may hold values from 0 to 32, as said below
- holder_table: int32 [32], P('groups'), parts along dimension 0, may hold values from 0 to 15, each once
Outputs:
- mixed: bfloat16 [4096, 1024], P(('groups', 'wide'), 'narrow'), parts along dimension 0
- down_gradient: bfloat16 [32, 8192, 64], P(('groups', 'wide'), 'narrow'), parts along dimension 0
- up_gradient: bfloat16 [32, 64, 1024], P(('groups', 'wide'), None, 'narrow'), parts along dimension 0
There are 2 independent parts, one for each index of `groups`. A program takes and returns all parts, laid end to end along the dimension named above; an argument that names none is the same for every part. Nothing has to cross between parts.
Inputs may be any that keep to these rules, and one draw needn't show every extreme that they name: counts[w, a] tokens of device w belong to adapter a and stand together in adapter order; each row sums to 256, and every row has an entry equal to 32. Adapter a's factors are row holder_table[a] of adapter_down and adapter_up, which lives on wide index holder_table[a] // 2.
All inputs are finite; a program needn't handle non-finite values.
Results may differ from a plain program's by a relative error of at most 0.005.
Values may be sent and summed in bfloat16 or wider, within the bound.
A program may use at most 64 MiB of HBM per device.

v0:
```python
import jax
import jax.numpy as jnp
from jax import lax
from jax.sharding import PartitionSpec as P

adapter_scale = 2.0


def body(tokens, output_gradient, value_weight, adapter_down, adapter_up, counts, holder_table):
    wide_count = lax.axis_size("wide")
    tok_rows = tokens.shape[0]
    resident_adapters = adapter_down.shape[0]
    all_adapters = resident_adapters * wide_count
    per_adapter = 2 * tok_rows // all_adapters
    row_counts = counts[0]
    group_ends = jnp.cumsum(row_counts)
    group_starts = group_ends - row_counts
    adapter_index = jnp.arange(all_adapters, dtype=jnp.int32)
    slot_table = (holder_table[None, :] == adapter_index[:, None]).astype(jnp.int32)
    slot_counts = jnp.dot(slot_table, row_counts)
    slot_starts = jnp.dot(slot_table, group_starts)
    offsets = jnp.arange(per_adapter, dtype=jnp.int32)
    valid = offsets[None, :] < slot_counts[:, None]
    source_rows = jnp.where(valid, slot_starts[:, None] + offsets[None, :], 0).reshape(-1)
    keep = valid.reshape(-1, 1)
    sent_tokens = jnp.where(
        keep, jnp.take(tokens, source_rows, axis=0), jnp.zeros((), tokens.dtype)
    )
    sent_grads = jnp.where(
        keep, jnp.take(output_gradient, source_rows, axis=0), jnp.zeros((), output_gradient.dtype)
    )
    sent_tokens = sent_tokens.reshape(wide_count, resident_adapters, per_adapter, tokens.shape[1])
    sent_grads = sent_grads.reshape(
        wide_count, resident_adapters, per_adapter, output_gradient.shape[1]
    )
    holder_tokens, holder_gradients = (
        lax.all_to_all(sent_tokens, "wide", split_axis=0, concat_axis=0, tiled=True),
        lax.all_to_all(sent_grads, "wide", split_axis=0, concat_axis=0, tiled=True),
    )
    down_part = jnp.einsum(
        "qopn,onx->qopx", holder_tokens, adapter_down, preferred_element_type=jnp.float32
    )
    up_piece = jnp.einsum(
        "gzme,zte->gzmt", holder_gradients, adapter_up, preferred_element_type=jnp.float32
    )
    rank_inputs, rank_outputs = lax.psum((down_part, up_piece), "narrow")
    in_low = rank_inputs.astype(jnp.bfloat16)
    out_low = rank_outputs.astype(jnp.bfloat16)
    down_gradient = (
        adapter_scale
        * jnp.einsum("wjkd,wjkr->jdr", holder_tokens, out_low, preferred_element_type=jnp.float32)
    ).astype(jnp.bfloat16)
    up_gradient = (
        adapter_scale
        * jnp.einsum("wjkr,wjkc->jrc", in_low, holder_gradients, preferred_element_type=jnp.float32)
    ).astype(jnp.bfloat16)
    token_pos = jnp.arange(tok_rows, dtype=jnp.int32)
    token_adapter = jnp.sum((group_ends[None, :] <= token_pos[:, None]).astype(jnp.int32), axis=1)
    token_table = (token_adapter[:, None] == adapter_index[None, :]).astype(jnp.int32)
    token_start = jnp.dot(token_table, group_starts)
    token_slot = jnp.dot(token_table, holder_table)
    back_rows = token_slot * per_adapter + token_pos - token_start
    base_part = jnp.dot(
        tokens,
        lax.all_gather(value_weight, "wide", axis=1, tiled=True),
        preferred_element_type=jnp.float32,
    )
    adapter_output = adapter_scale * jnp.einsum(
        "mpea,pai->mpei",
        rank_inputs,
        adapter_up.astype(jnp.float32),
        precision=lax.Precision.HIGHEST,
    )
    came_home = lax.all_to_all(adapter_output, "wide", split_axis=0, concat_axis=0, tiled=True)
    adapter_rows = jnp.take(
        came_home.reshape(all_adapters * per_adapter, came_home.shape[3]), back_rows, axis=0
    )
    combined_sum = lax.psum_scatter(base_part, "narrow", scatter_dimension=1, tiled=True)
    mixed = (combined_sum + adapter_rows).astype(jnp.bfloat16)
    return (mixed, down_gradient, up_gradient)


def solution(mesh):
    in_specs = (
        P(("groups", "wide"), "narrow"),
        P(("groups", "wide"), "narrow"),
        P("narrow", "wide"),
        P(("groups", "wide"), "narrow", None),
        P(("groups", "wide"), None, "narrow"),
        P(("groups", "wide"), None),
        P("groups"),
    )
    out_specs = (
        P(("groups", "wide"), "narrow"),
        P(("groups", "wide"), "narrow", None),
        P(("groups", "wide"), None, "narrow"),
    )
    return jax.shard_map(body, mesh=mesh, in_specs=in_specs, out_specs=out_specs, check_vma=False)
```

profile of v0, /device:TPU:0, one launch (start us, length us, event | category | flops | bytes accessed | tf_op | source)
XLA Modules:
  0.0 281.2 jit_solution(14232925878315155103)
XLA Ops:
  8.0 0.0 copy-start
  8.0 0.0 all-gather.2.cloned.1.call-start
  8.1 0.7 all-gather.2.cloned.1.call-update
  8.7 0.7 copy.25
  9.5 0.1 reduce
  9.6 0.8 convolution_bitcast_fusion.4
  10.4 0.1 lt.73
  10.5 0.8 convolution_bitcast_fusion.3
  11.3 0.1 add.78
  11.4 0.1 add_select_fusion
  11.5 0.1 select_n.72
  11.6 0.0 copy-done
  11.6 4.4 %gather_fusion = bf16[512,4096]{1,0:T(8,128)(2,1)} fusion(bf16[256,4096]{1,0:T(8,128)(2,1)S(1)} %copy-done, s32[1024]{0:T(1024)S(1)} %pad_clamp_fusion.1), kind=kCustom, calls=%fused_computation | custom fusion | bytes 8390656 | tf_op jit(solution)/shard_map/jit(_take)/gather | solution.py:27
  16.0 0.1 iota_compare_fusion.8
  16.1 3.9 %select_select_fusion = bf16[8,2,32,4096]{3,2,1,0:T(8,128)(2,1)} fusion(bf16[8,2,32,4096]{3,2,1,0:T(8,128)(2,1)} %bitcast.64, pred[8,2,32]{2,1,0:T(4,128)(4,1)S(1)} %get-tuple-element.6, pred[8,2,32]{2,1,0:T(4,128)(4,1)S(1)} %get-tuple-element.5), kind=kLoop, calls=%fused_computation.8 | loop fusion | flops 4194304 | bytes 8389632 | tf_op jit(solution)/shard_map/jit(_where)/select_n | solution.py:26
  20.0 7.4 %all-to-all-start = ((bf16[8,2,32,4096]{3,2,1,0:T(8,128)(2,1)}), bf16[8,2,32,4096]{3,2,1,0:T(8,128)(2,1)}, u32[]{:S(2)}, u32[]{:S(2)}) async-start(bf16[8,2,32,4096]{3,2,1,0:T(8,128)(2,1)} %select_select_fusion), calls=%async_computation.1 | async-start | bytes 8388608 | tf_op jit(solution)/shard_map/all_to_all | solution.py:37
  27.4 0.0 copy-done.1
  27.4 2.0 gather_fusion.2
  29.4 1.0 select_select_fusion.1
  30.4 153.8 %all-to-all-done = bf16[8,2,32,4096]{3,2,1,0:T(8,128)(2,1)} async-done(((bf16[8,2,32,4096]{3,2,1,0:T(8,128)(2,1)}), bf16[8,2,32,4096]{3,2,1,0:T(8,128)(2,1)}, u32[]{:S(2)}, u32[]{:S(2)}) %all-to-all-start) | async-done | bytes 4194336 | tf_op jit(solution)/shard_map/all_to_all | solution.py:37
  184.2 3.5 %all-to-all-start.2 = ((bf16[8,2,32,512]{3,2,1,0:T(8,128)(2,1)}), bf16[8,2,32,512]{3,2,1,0:T(8,128)(2,1)S(1)}, u32[]{:S(2)}, u32[]{:S(2)}) async-start(bf16[8,2,32,512]{3,2,1,0:T(8,128)(2,1)} %select_select_fusion.1), calls=%async_computation.3 | async-start | bytes 1048576 | tf_op jit(solution)/shard_map/all_to_all | solution.py:38
  187.7 0.0 all-reduce.3.cloned.1.call-start
  187.7 4.5 %fusion.5 = f32[8,2,32,64]{3,2,0,1:T(8,128)} fusion(bf16[8,2,32,4096]{3,2,1,0:T(8,128)(2,1)} %all-to-all-done, bf16[2,4096,64]{1,2,0:T(8,128)(2,1)} %param.10), kind=kOutput, calls=%fused_computation.11 | convolution fusion | flops 268435456 | bytes 5373952 | tf_op jit(solution)/shard_map/qopn,onx->qopx/dot_general | solution.py:40
  192.3 0.0 all-reduce.3.cloned.1.call-update
  192.3 0.0 copy-start.5
  192.3 0.0 reduce-scatter.2.cloned.1.call-start
  192.3 37.1 %all-gather.2.cloned.1.call-done = bf16[4096,1024]{1,0:T(8,128)(2,1)} async-done(((bf16[4096,128]{1,0:T(8,128)(2,1)}), bf16[4096,1024]{1,0:T(8,128)(2,1)}) %all-gather.2.cloned.1.call-update) | async-done | bytes 8388624 | tf_op jit(solution)/shard_map/all_gather | solution.py:65
  229.5 6.7 %fusion.28 = f32[256,1024]{1,0:T(8,128)} fusion(bf16[256,4096]{1,0:T(8,128)(2,1)S(1)} %copy-done, bf16[4096,1024]{1,0:T(8,128)(2,1)} %all-gather.2.cloned.1.call-done), kind=kOutput, calls=%fused_computation.51 | convolution fusion | flops 2147483648 | bytes 11534336 | tf_op jit(solution)/shard_map/dot_general | solution.py:63
  236.2 0.0 reduce-scatter.2.cloned.1.call-update
  236.2 0.0 all-reduce.3.cloned.1.call-done
  236.3 0.0 copy-done.5
  236.3 1.5 fusion.4
  237.8 1.1 copy.27
  238.9 0.0 all-to-all-done.2
  238.9 0.8 copy-done.2
  239.7 4.4 %all-to-all-start.1 = ((f32[8,2,32,512]{3,2,1,0:T(8,128)}), f32[8,2,32,512]{3,2,1,0:T(8,128)S(1)}, u32[]{:S(2)}, u32[]{:S(2)}) async-start(f32[8,2,32,512]{3,2,1,0:T(8,128)} %copy.27), calls=%async_computation.2 | async-start | bytes 2097152 | tf_op jit(solution)/shard_map/all_to_all | solution.py:74
  244.0 0.1 convert_reduce_fusion
  244.1 0.2 fusion.18
  244.4 0.0 copy-done.6
  244.4 0.3 fusion.17
  244.7 2.0 convolution_bitcast_fusion.2
  246.7 4.9 %all-reduce.4 = bf16[8,2,32,64]{3,2,0,1:T(8,128)(2,1)S(1)} all-reduce(f32[8,2,32,64]{3,2,0,1:T(8,128)} %convolution_bitcast_fusion.2), channel_id=1, replica_groups=mesh['groups'=2,'wide'=8,'narrow'=2] {'narrow'}, use_global_device_ids=true, to_apply=%region_4.5 | all-reduce | flops 32768 | bytes 196608 | tf_op jit(solution)/shard_map/psum | solution.py:46
  251.6 4.1 %fusion.1 = bf16[2,4096,64]{1,2,0:T(8,128)(2,1)} fusion(bf16[8,2,32,4096]{3,2,1,0:T(8,128)(2,1)} %all-to-all-done, bf16[8,2,32,64]{3,2,0,1:T(8,128)(2,1)S(1)} %all-reduce.4), kind=kOutput, calls=%fused_computation.5 | convolution fusion | flops 269484032 | bytes 5308416 | tf_op jit(solution)/shard_map/wjkd,wjkr->jdr/dot_general | solution.py:51
  255.8 0.0 copy-done.3
  255.8 0.9 fusion.9
  256.7 13.3 %all-to-all-done.1 = f32[8,2,32,512]{3,2,1,0:T(8,128)S(1)} async-done(((f32[8,2,32,512]{3,2,1,0:T(8,128)}), f32[8,2,32,512]{3,2,1,0:T(8,128)S(1)}, u32[]{:S(2)}, u32[]{:S(2)}) %all-to-all-start.1) | async-done | bytes 1048608 | tf_op jit(solution)/shard_map/all_to_all | solution.py:74
  269.9 1.8 gather_fusion.1
  271.7 2.0 add_convert_fusion
  (14 shorter events, 0.1 us)
Async XLA Ops:
  8.0 3.6 %copy-start = (bf16[256,4096]{1,0:T(8,128)(2,1)S(1)}, bf16[256,4096]{1,0:T(8,128)(2,1)}, u32[]{:S(2)}) copy-start(bf16[256,4096]{1,0:T(8,128)(2,1)} %param.7) | copy-start | bytes 6291460
  8.0 221.4 %all-gather.2.cloned.1.call-start = ((), (), s32[]{:S(2)}) async-start(), calls=%async_computation.4 | async-start | bytes 9437184 | tf_op jit(solution)/shard_map/all_gather | solution.py:65
  20.0 7.4 %copy-start.1 = (bf16[256,512]{1,0:T(8,128)(2,1)S(1)}, bf16[256,512]{1,0:T(8,128)(2,1)}, u32[]{:S(2)}) copy-start(bf16[256,512]{1,0:T(8,128)(2,1)} %param.8) | copy-start | bytes 786436
  20.0 164.2 %all-to-all-start = ((bf16[8,2,32,4096]{3,2,1,0:T(8,128)(2,1)}), bf16[8,2,32,4096]{3,2,1,0:T(8,128)(2,1)}, u32[]{:S(2)}, u32[]{:S(2)}) async-start(bf16[8,2,32,4096]{3,2,1,0:T(8,128)(2,1)} %select_select_fusion), calls=%async_computation.1 | async-start | bytes 8388608 | tf_op jit(solution)/shard_map/all_to_all | solution.py:37
  184.2 54.7 %all-to-all-start.2 = ((bf16[8,2,32,512]{3,2,1,0:T(8,128)(2,1)}), bf16[8,2,32,512]{3,2,1,0:T(8,128)(2,1)S(1)}, u32[]{:S(2)}, u32[]{:S(2)}) async-start(bf16[8,2,32,512]{3,2,1,0:T(8,128)(2,1)} %select_select_fusion.1), calls=%async_computation.3 | async-start | bytes 1048576 | tf_op jit(solution)/shard_map/all_to_all | solution.py:38
  187.7 48.6 %all-reduce.3.cloned.1.call-start = ((), (), s32[]{:S(2)}) async-start(), calls=%async_computation.6 | async-start | bytes 524288 | tf_op jit(solution)/shard_map/psum | solution.py:46
  192.3 44.0 %copy-start.5 = (bf16[2,64,512]{2,1,0:T(8,128)(2,1)S(1)}, bf16[2,64,512]{2,1,0:T(8,128)(2,1)}, u32[]{:S(2)}) copy-start(bf16[2,64,512]{2,1,0:T(8,128)(2,1)} %param.11) | copy-start | bytes 393220
  192.3 79.4 %reduce-scatter.2.cloned.1.call-start = ((), (), s32[]{:S(2)}) async-start(), calls=%async_computation.5 | async-start | bytes 1572864 | tf_op jit(solution)/shard_map/reduce_scatter | solution.py:78
  236.2 7.9 %copy-start.7 = (s32[16]{0:T(128)S(1)}, s32[16]{0:T(128)}, u32[]{:S(2)}) copy-start(s32[16]{0:T(128)} %param.13) | copy-start | bytes 196
  236.2 8.2 %copy-start.6 = (s32[1,16]{1,0:T(1,128)S(1)}, s32[1,16]{1,0:T(1,128)}, u32[]{:S(2)}) copy-start(s32[1,16]{1,0:T(1,128)} %param.12) | copy-start | bytes 196
  238.8 16.9 %copy-start.4 = (f32[8,2,32,64]{3,2,0,1:T(8,128)S(1)}, f32[8,2,32,64]{3,2,0,1:T(8,128)}, u32[]{:S(2)}) copy-start(f32[8,2,32,64]{3,2,0,1:T(8,128)} %all-reduce.3.cloned.1.call-done) | copy-start | bytes 393220
  238.9 0.8 copy-start.2
  239.7 30.3 %all-to-all-start.1 = ((f32[8,2,32,512]{3,2,1,0:T(8,128)}), f32[8,2,32,512]{3,2,1,0:T(8,128)S(1)}, u32[]{:S(2)}, u32[]{:S(2)}) async-start(f32[8,2,32,512]{3,2,1,0:T(8,128)} %copy.27), calls=%async_computation.2 | async-start | bytes 2097152 | tf_op jit(solution)/shard_map/all_to_all | solution.py:74
  251.6 4.1 %copy-start.3 = (bf16[8,2,32,512]{3,2,1,0:T(8,128)(2,1)S(1)}, bf16[8,2,32,512]{3,2,1,0:T(8,128)(2,1)}, u32[]{:S(2)}) copy-start(bf16[8,2,32,512]{3,2,1,0:T(8,128)(2,1)} %copy-done.2) | copy-start | bytes 1572868
Sparse Core Ops, SparseCore 0:
  11.1 218.3 all-gather.1
Sparse Core Ops, SparseCore 1:
  192.4 18.8 all-reduce.2
  236.3 8.3 reduce-scatter.1
where the time goes:
time: 282 us; the launch traced here: 281 us
  waiting for transfers between devices  205 us (73%)
  matrix products  21.9 us (8%)
  between operations  15.6 us (6%)
  starting transfers between devices  15.5 us (5%)
  local copies, waits for them, and re-layouts  11 us (4%)
  other arithmetic  7.37 us (3%)
  blocking collectives  4.91 us (2%)
    all_to_all x1, waiting for transfers between devices, body(): lax.all_to_all(sent_tokens, 'wide', split_axis=0, concat_axis=0, tiled=True)  154 us
    all_gather x1, waiting for transfers between devices, body(): lax.all_gather(value_weight, 'wide', axis=1, tiled=True)  37.1 us
    all_to_all x1, waiting for transfers between devices, body(): lax.all_to_all(adapter_output, 'wide', split_axis=0, concat_axis=0, tiled...  13.3 us
    all_to_all x1, starting transfers between devices, body(): lax.all_to_all(sent_tokens, 'wide', split_axis=0, concat_axis=0, tiled=True)  7.44 us
    dot_general x1, matrix products, body(): jnp.dot(tokens, lax.all_gather(value_weight, 'wide', axis=1, tiled=True),...  6.74 us
  transfers between devices with their start and end apart: 6, of which 3 were waited for; matrix products, arithmetic and copies ran while one was open for 13% of the time, Pallas kernels for 0%

commit v1 on v0

--- a/solution.py
+++ b/solution.py
@@ -1,12 +1,17 @@
 import jax
 import jax.numpy as jnp
 from jax import lax
+from jax.experimental import pallas as pl
+from jax.experimental.pallas import tpu as pltpu
 from jax.sharding import PartitionSpec as P
 
+MESH = pl.DeviceIdType.MESH
+PIECES = 4
+
 adapter_scale = 2.0
 
 
-def body(tokens, output_gradient, value_weight, adapter_down, adapter_up, counts, holder_table):
+def plain_body(tokens, output_gradient, value_weight, adapter_down, adapter_up, counts, holder_table):
     wide_count = lax.axis_size("wide")
     tok_rows = tokens.shape[0]
     resident_adapters = adapter_down.shape[0]
@@ -80,6 +85,266 @@
     return (mixed, down_gradient, up_gradient)
 
 
+def exchange_kernel(
+    weight, tokens, sent_tok, sent_grad,
+    base, got_tok, got_grad,
+    blocks, tok, acc, keep_own, keep_far, from_core, from_group,
+    up_s, up_r, down_s, down_r, side_s, side_r, local, tok_s, tok_r, grad_s, grad_r, one_s, one_r,
+):
+    group = lax.axis_index("groups")
+    me = lax.axis_index("wide")
+    core = lax.axis_index("narrow")
+    z, x = me // 2, me % 2
+    depth = tok.shape[2]
+    rows = depth // PIECES
+
+    barrier = pltpu.get_barrier_semaphore()
+    for k in range(1, 8):
+        pl.semaphore_signal(barrier, inc=1, device_id={"wide": me ^ k}, device_id_type=MESH)
+    pl.semaphore_signal(barrier, inc=1, device_id={"narrow": 1 - core}, device_id_type=MESH)
+    pl.semaphore_signal(barrier, inc=1, device_id={"groups": 1 - group}, device_id_type=MESH)
+    pl.semaphore_wait(barrier, 9)
+
+    def step(first, slot, c, target, send, recv):
+        there = blocks.at[slot, pl.ds(c * rows, rows)]
+        here = weight.at[pl.ds(group * depth + c * rows, rows)] if first else there
+        return pltpu.make_async_remote_copy(
+            src_ref=here, dst_ref=there, send_sem=send, recv_sem=recv,
+            device_id={"wide": target}, device_id_type=MESH,
+        )
+
+    for c in range(PIECES):
+        @pl.when(z < 3)
+        def _():
+            step(True, me, c, me + 2, up_s.at[z, c], up_r.at[z, c]).start()
+
+        @pl.when(z > 0)
+        def _():
+            step(True, me, c, me - 2, down_s.at[z, c], down_r.at[z, c]).start()
+
+        step(True, me, c, me ^ 1, side_s.at[z, c], side_r.at[z, c]).start()
+
+    far_tok = pltpu.make_async_remote_copy(
+        src_ref=tokens.at[:, pl.ds((1 - group) * depth, depth)], dst_ref=tok.at[1],
+        send_sem=one_s.at[0], recv_sem=one_r.at[0],
+        device_id={"groups": 1 - group}, device_id_type=MESH,
+    )
+    far_tok.start()
+    own = [
+        pltpu.make_async_copy(
+            weight.at[pl.ds(group * depth, depth)], blocks.at[me], local.at[0]),
+        pltpu.make_async_copy(
+            tokens.at[:, pl.ds(group * depth, depth)], tok.at[0], local.at[1]),
+        pltpu.make_async_copy(sent_tok.at[me], got_tok.at[me], local.at[2]),
+        pltpu.make_async_copy(sent_grad.at[me], got_grad.at[me], local.at[3]),
+    ]
+    for copy in own:
+        copy.start()
+
+    routed = []
+    for k in range(1, 8):
+        for src, dst, send, recv in (
+            (sent_grad, got_grad, grad_s, grad_r), (sent_tok, got_tok, tok_s, tok_r)
+        ):
+            copy = pltpu.make_async_remote_copy(
+                src_ref=src.at[me ^ k], dst_ref=dst.at[me],
+                send_sem=send.at[k], recv_sem=recv.at[k],
+                device_id={"wide": me ^ k}, device_id_type=MESH,
+            )
+            copy.start()
+            routed.append(copy)
+
+    for d in range(1, 4):
+        for c in range(PIECES):
+            @pl.when(z >= d)
+            def _():
+                at = z - d
+                slot = 2 * at + x
+                step(False, slot, c, me ^ 1, up_s.at[at, c], up_r.at[at, c]).wait_recv()
+
+                @pl.when(z < 3)
+                def _():
+                    step(False, slot, c, me + 2, up_s.at[at, c], up_r.at[at, c]).start()
+
+                step(False, slot, c, me ^ 1, side_s.at[at, c], side_r.at[at, c]).start()
+
+            @pl.when(z + d < 4)
+            def _():
+                at = z + d
+                slot = 2 * at + x
+                step(False, slot, c, me ^ 1, down_s.at[at, c], down_r.at[at, c]).wait_recv()
+
+                @pl.when(z > 0)
+                def _():
+                    step(False, slot, c, me - 2, down_s.at[at, c], down_r.at[at, c]).start()
+
+                step(False, slot, c, me ^ 1, side_s.at[at, c], side_r.at[at, c]).start()
+
+    for at in range(4):
+        for c in range(PIECES):
+            step(False, 2 * at + 1 - x, c, me ^ 1, side_s.at[at, c], side_r.at[at, c]).wait_recv()
+    own[0].wait()
+    own[1].wait()
+    far_tok.wait_recv()
+
+    both = tok[...].reshape(tok.shape[0] * tok.shape[1], depth)
+
+    def column(w, carry):
+        acc[w] = jnp.dot(both, blocks[w], preferred_element_type=jnp.float32)
+        return carry
+
+    lax.fori_loop(0, 8, column, 0)
+    to_core = pltpu.make_async_remote_copy(
+        src_ref=acc.at[pl.ds(4 * (1 - core), 4)], dst_ref=from_core,
+        send_sem=one_s.at[1], recv_sem=one_r.at[1],
+        device_id={"narrow": 1 - core}, device_id_type=MESH,
+    )
+    to_core.start()
+    to_core.wait_recv()
+    count = tok.shape[1]
+    keep_far[...] = acc[pl.ds(4 * core, 4), count:] + from_core[:, count:]
+    to_group = pltpu.make_async_remote_copy(
+        src_ref=keep_far, dst_ref=from_group,
+        send_sem=one_s.at[2], recv_sem=one_r.at[2],
+        device_id={"groups": 1 - group}, device_id_type=MESH,
+    )
+    to_group.start()
+    keep_own[...] = acc[pl.ds(4 * core, 4), :count] + from_core[:, :count]
+    to_group.wait_recv()
+    for w in range(4):
+        base[:, w * 128 : (w + 1) * 128] = keep_own[w] + from_group[w]
+
+    far_tok.wait_send()
+    to_core.wait_send()
+    to_group.wait_send()
+    for at in range(4):
+        for c in range(PIECES):
+            step(False, 2 * at + x, c, me ^ 1, side_s.at[at, c], side_r.at[at, c]).wait_send()
+
+            @pl.when((at <= z) & (z < 3))
+            def _():
+                step(False, 2 * at + x, c, me ^ 1, up_s.at[at, c], up_r.at[at, c]).wait_send()
+
+            @pl.when((at >= z) & (z > 0))
+            def _():
+                step(False, 2 * at + x, c, me ^ 1, down_s.at[at, c], down_r.at[at, c]).wait_send()
+    own[2].wait()
+    own[3].wait()
+    for copy in routed:
+        copy.wait()
+
+
+def exchange(weight, tokens, sent_tok, sent_grad):
+    count, width = tokens.shape
+    half = width // 2
+    out_columns = weight.shape[1] * 4
+    anywhere = pl.BlockSpec(memory_space=pl.ANY)
+    dma = pltpu.SemaphoreType.DMA
+    return pl.pallas_call(
+        exchange_kernel,
+        out_shape=(
+            jax.ShapeDtypeStruct((count, out_columns), jnp.float32),
+            jax.ShapeDtypeStruct(sent_tok.shape, sent_tok.dtype),
+            jax.ShapeDtypeStruct(sent_grad.shape, sent_grad.dtype),
+        ),
+        in_specs=[anywhere] * 4,
+        out_specs=(pl.BlockSpec(memory_space=pltpu.VMEM), anywhere, anywhere),
+        scratch_shapes=[
+            pltpu.VMEM((8, half, 128), jnp.bfloat16),
+            pltpu.VMEM((2, count, half), jnp.bfloat16),
+            pltpu.VMEM((8, 2 * count, 128), jnp.float32),
+            pltpu.VMEM((4, count, 128), jnp.float32),
+            pltpu.VMEM((4, count, 128), jnp.float32),
+            pltpu.VMEM((4, 2 * count, 128), jnp.float32),
+            pltpu.VMEM((4, count, 128), jnp.float32),
+        ]
+        + [dma((4, PIECES))] * 6
+        + [dma((4,))]
+        + [dma((8,))] * 4
+        + [dma((3,))] * 2,
+        compiler_params=pltpu.CompilerParams(
+            collective_id=0, has_side_effects=True, vmem_limit_bytes=40 * 1024 * 1024
+        ),
+        cost_estimate=pl.CostEstimate(
+            flops=2 * 512 * 2048 * 1024, bytes_accessed=40 * 1024 * 1024, transcendentals=0
+        ),
+    )(weight, tokens, sent_tok, sent_grad)
+
+
+def over_cores(value):
+    return value + lax.ppermute(value, "narrow", [(0, 1), (1, 0)])
+
+
+def fused_body(
+    tokens, output_gradient, value_weight, adapter_down, adapter_up, counts, holder_table
+):
+    exact = lax.Precision.HIGHEST
+    wide_count = lax.axis_size("wide")
+    tok_rows = tokens.shape[0]
+    resident = adapter_down.shape[0]
+    adapters = resident * wide_count
+    per_adapter = 2 * tok_rows // adapters
+    rank = adapter_down.shape[2]
+    row_counts = counts[0]
+    index = jnp.arange(adapters, dtype=jnp.int32)
+    before = (index[None, :] < index[:, None]).astype(jnp.int32)
+    starts = jnp.sum(before * row_counts[None, :], axis=1)
+    slot_table = (holder_table[None, :] == index[:, None]).astype(jnp.int32)
+    slot_counts = jnp.sum(slot_table * row_counts[None, :], axis=1)
+    slot_starts = jnp.sum(slot_table * starts[None, :], axis=1)
+    offset = jnp.arange(per_adapter, dtype=jnp.int32)
+    position = jnp.arange(tok_rows, dtype=jnp.int32)
+    source = jnp.where(
+        offset[None, :] < slot_counts[:, None], slot_starts[:, None] + offset[None, :], -1
+    )
+    pick = source[:, :, None] == position[None, None, :]
+    pick = pick.reshape(adapters * per_adapter, tok_rows)
+    pick_low = pick.astype(jnp.bfloat16)
+    sent_tok = jnp.dot(pick_low, tokens, preferred_element_type=jnp.bfloat16)
+    sent_grad = jnp.dot(pick_low, output_gradient, preferred_element_type=jnp.bfloat16)
+    all_up = lax.all_gather(adapter_up, "wide", axis=0, tiled=True)
+    base, got_tok, got_grad = exchange(
+        value_weight,
+        tokens,
+        sent_tok.reshape(wide_count, resident * per_adapter, -1),
+        sent_grad.reshape(wide_count, resident * per_adapter, -1),
+    )
+    got_tok = got_tok.reshape(wide_count, resident, per_adapter, -1)
+    got_grad = got_grad.reshape(wide_count, resident, per_adapter, -1)
+    rank_in = over_cores(
+        jnp.einsum("qopn,onx->qopx", got_tok, adapter_down, preferred_element_type=jnp.float32)
+    )
+    rank_out = over_cores(
+        jnp.einsum("gzme,zte->gzmt", got_grad, adapter_up, preferred_element_type=jnp.float32)
+    )
+    home = lax.all_to_all(rank_in, "wide", split_axis=0, concat_axis=0, tiled=True)
+    in_low = rank_in.astype(jnp.bfloat16)
+    out_low = rank_out.astype(jnp.bfloat16)
+    down_gradient = (
+        adapter_scale
+        * jnp.einsum("wjkd,wjkr->jdr", got_tok, out_low, preferred_element_type=jnp.float32)
+    ).astype(jnp.bfloat16)
+    up_gradient = (
+        adapter_scale
+        * jnp.einsum("wjkr,wjkc->jrc", in_low, got_grad, preferred_element_type=jnp.float32)
+    ).astype(jnp.bfloat16)
+    ranks = lax.dot_general(
+        pick.astype(jnp.float32), home.reshape(adapters * per_adapter, rank),
+        (((0,), (0,)), ((), ())), precision=exact,
+    )
+    owner = (position[:, None] >= slot_starts[None, :]) & (
+        position[:, None] < (slot_starts + slot_counts)[None, :]
+    )
+    spread = jnp.where(owner[:, :, None], ranks[:, None, :], 0.0)
+    lora = jnp.dot(
+        spread.reshape(tok_rows, adapters * rank),
+        all_up.reshape(adapters * rank, -1).astype(jnp.float32),
+        precision=exact,
+    )
+    mixed = (base + adapter_scale * lora).astype(jnp.bfloat16)
+    return (mixed, down_gradient, up_gradient)
+
+
 def solution(mesh):
     in_specs = (
         P(("groups", "wide"), "narrow"),
@@ -95,4 +360,7 @@
         P(("groups", "wide"), "narrow", None),
         P(("groups", "wide"), None, "narrow"),
     )
+    shape = mesh.shape
+    small = (shape["groups"], shape["wide"], shape["narrow"]) == (2, 8, 2)
+    body = fused_body if small else plain_body
     return jax.shard_map(body, mesh=mesh, in_specs=in_specs, out_specs=out_specs, check_vma=False)

time: 282 us -> 215 us (0.76)
  waiting for transfers between devices: 205 us -> 3.78 us
  Pallas kernels: 0 us -> 172 us
  starting transfers between devices: 15.5 us -> 6.4 us
  local copies, waits for them, and re-layouts: 11 us -> 2.16 us
  matrix products: 21.9 us -> 13.2 us
  blocking collectives: 4.91 us -> 0 us
  other arithmetic: 7.37 us -> 2.74 us
    pallas_call x0 -> x1, Pallas kernels: none -> 172 us  [exchange(): pl.pallas_call(exchange_kernel, out_shape=(jax.ShapeDtypeStruct((count, o...]
    all_to_all x3 -> x1, waiting for transfers between devices: 167 us -> 2.54 us  [fused_body(): lax.all_to_all(rank_in, 'wide', split_axis=0, concat_axis=0, tiled=True)]
    all_gather x1, waiting for transfers between devices: 37.1 us -> 0.02 us  [fused_body(): all_up = lax.all_gather(adapter_up, 'wide', axis=0, tiled=True)]
    all_to_all x3 -> x1, starting transfers between devices: 15.3 us -> 4.63 us  [fused_body(): lax.all_to_all(rank_in, 'wide', split_axis=0, concat_axis=0, tiled=True)]
    dot_general x10 -> x8, matrix products: 21.9 us -> 13.2 us  [the longest x1 4.05 us: fused_body(): jnp.einsum('wjkd,wjkr->jdr', got_tok, out_low, preferred_element_type=jnp...]
    gather x3 -> x0, local copies, waits for them, and re-layouts: 8.11 us -> none  [the longest x1 4.39 us: body(): jnp.take(tokens, source_rows, axis=0)]
    psum x1 -> x0, blocking collectives: 4.91 us -> none  [body(): rank_inputs, rank_outputs = lax.psum((down_part, up_piece), 'narrow')]
    select_n x4 -> x2, other arithmetic: 4.96 us -> 0.08 us  [fused_body(): jnp.where(offset[None, :] < slot_counts[:, None], slot_starts[:, None] +...]
  transfers between devices with their start and end apart: 6 -> 4, of which waited for: 3 -> 2; matrix products, arithmetic and copies ran while one was open for 13% -> 7% of each run, Pallas kernels for 0% -> 80%
where the time goes in v1:
time: 215 us
  Pallas kernels  172 us (80%)
  between operations  14.2 us (7%)
  matrix products  13.2 us (6%)
  starting transfers between devices  6.4 us (3%)
  waiting for transfers between devices  3.78 us (2%)
  other arithmetic  2.74 us (1%)
  local copies, waits for them, and re-layouts  2.16 us (1%)
    pallas_call x1, Pallas kernels, exchange(): pl.pallas_call(exchange_kernel, out_shape=(jax.ShapeDtypeStruct((count, o...  172 us
    all_to_all x1, starting transfers between devices, fused_body(): lax.all_to_all(rank_in, 'wide', split_axis=0, concat_axis=0, tiled=True)  4.63 us
  transfers between devices with their start and end apart: 4, of which 2 were waited for; matrix products, arithmetic and copies ran while one was open for 7% of the time, Pallas kernels for 80%

profile of v1, /device:TPU:0, one launch (start us, length us, event | category | flops | bytes accessed | tf_op | source)
XLA Modules:
  0.0 214.6 jit_solution(15630955517659933571)
XLA Ops:
  7.2 0.0 copy-start
  7.2 0.0 copy-start.2
  7.2 0.0 copy-start.8
  7.2 0.0 all-gather.2.cloned.1.call-start
  7.2 0.7 all-gather.2.cloned.1.call-update
  7.9 0.8 select_reduce_fusion.1
  8.7 0.8 select_reduce_fusion.2
  9.5 0.1 add.41
  9.6 0.1 add.42
  9.7 0.1 add.43
  9.8 0.1 lt.70
  9.9 0.1 lt.71
  9.9 0.1 lt.72
  10.0 0.1 lt.68
  10.1 3.0 %fusion.4.sent_tok = bf16[8,64,4096]{2,1,0:T(8,128)(2,1)S(1)} fusion(bf16[256,4096]{1,0:T(8,128)(2,1)} %tokens.1, s32[8,64]{1,0:T(8,128)S(1)} %add_select_fusion.1), kind=kOutput, calls=%fused_computation.5 | convolution fusion | flops 1073872896 | bytes 6293504 | tf_op jit(solution)/shard_map/dot_general | solution.py:303
  13.1 0.0 copy-done.8
  13.1 0.3 fusion.18.sent_grad
  13.5 0.0 copy-done.2
  13.5 0.0 copy-done.5
  13.5 172.1 %shard_map.94 = (f32[256,512]{1,0:T(8,128)S(1)}, bf16[8,64,4096]{2,1,0:T(8,128)(2,1)S(1)}, bf16[8,64,512]{2,1,0:T(8,128)(2,1)S(1)}) custom-call(bf16[4096,128]{1,0:T(8,128)(2,1)S(1)} %copy-done.5, bf16[256,4096]{1,0:T(8,128)(2,1)S(1)} %copy-done.2, bf16[8,64,4096]{2,1,0:T(8,128)(2,1)S(1)} %fusion.4.sent_tok, bf16[8,64,512]{2,1,0:T(8,128)(2,1)S(1)} %fusion.18.sent_grad), custom_call_target="tpu_custom_call" | custom-call | flops 2147483648 | bytes 41943040 | tf_op jit(solution)/shard_map/pallas_call | solution.py:243
  185.6 0.0 copy-start.1
  185.6 0.0 copy-start.3
  185.6 0.0 copy-start.6
  185.6 0.0 copy-start.9
  185.6 0.0 copy-done
  185.7 1.2 fusion.9
  186.9 1.6 collective-permute-start
  188.5 0.0 copy-done.9
  188.5 0.3 convolution_bitcast_fusion.3
  188.8 0.1 collective-permute-start.1
  188.9 0.0 copy-done.1
  188.9 0.1 add_select_fusion
  189.0 0.1 select_n.20
  189.1 0.1 fusion.30
  189.2 0.5 collective-permute-done
  189.8 0.8 reshape.149
  190.6 4.6 %all-to-all-start = ((f32[8,1,4096]{2,1,0:T(1,128)}), f32[8,1,4096]{2,1,0:T(1,128)S(1)}, u32[]{:S(2)}, u32[]{:S(2)}) async-start(f32[8,1,4096]{2,1,0:T(1,128)} %reshape.149), calls=%async_computation | async-start | bytes 262144 | tf_op jit(solution)/shard_map/all_to_all | solution.py:320
  195.2 0.0 collective-permute-done.1
  195.2 4.1 %fusion.1 = bf16[2,4096,64]{1,2,0:T(8,128)(2,1)} fusion(bf16[8,2,32,4096]{3,2,1,0:T(8,128)(2,1)} %bitcast.49, f32[8,2,32,64]{3,2,0,1:T(8,128)S(1)} %convolution_bitcast_fusion.3, f32[8,2,32,64]{3,2,0,1:T(8,128)S(1)} %collective-permute-done.1), kind=kOutput, calls=%fused_computation.2 | convolution fusion | flops 269549568 | bytes 5505024 | tf_op jit(solution)/shard_map/wjkd,wjkr->jdr/dot_general | solution.py:325
  199.3 0.0 copy-done.4
  199.3 0.9 fusion.13
  200.2 2.5 %all-to-all-done = f32[8,1,4096]{2,1,0:T(1,128)S(1)} async-done(((f32[8,1,4096]{2,1,0:T(1,128)}), f32[8,1,4096]{2,1,0:T(1,128)S(1)}, u32[]{:S(2)}, u32[]{:S(2)}) %all-to-all-start) | async-done | bytes 131104 | tf_op jit(solution)/shard_map/all_to_all | solution.py:320
  202.7 0.5 broadcast.87
  203.3 1.0 reduce
  204.2 0.1 reshape.150
  204.3 0.5 fusion.19
  204.8 0.0 all-gather.2.cloned.1.call-done
  204.8 3.0 %fusion.8 = bf16[256,512]{1,0:T(8,128)(2,1)} fusion(f32[256,512]{1,0:T(8,128)S(1)} %copy-done.7, bf16[16,64,512]{2,1,0:T(8,128)(2,1)} %all-gather.2.cloned.1.call-done, f32[256,64]{0,1:T(8,128)S(1)} %fusion.19, pred[256,16]{0,1:T(8,128)(4,1)S(1)} %fusion.30), kind=kOutput, calls=%fused_computation.10 | convolution fusion | flops 1611268096 | bytes 1904640 | tf_op jit(solution)/shard_map/dot_general | solution.py:339
  (11 shorter events, 0.1 us)
Async XLA Ops:
  7.2 178.5 %copy-start = (bf16[2,4096,64]{1,2,0:T(8,128)(2,1)S(1)}, bf16[2,4096,64]{1,2,0:T(8,128)(2,1)}, u32[]{:S(2)}) copy-start(bf16[2,4096,64]{1,2,0:T(8,128)(2,1)} %param.10) | copy-start | bytes 3145732
  7.2 6.3 %copy-start.2 = (bf16[256,4096]{1,0:T(8,128)(2,1)S(1)}, bf16[256,4096]{1,0:T(8,128)(2,1)}, u32[]{:S(2)}) copy-start(bf16[256,4096]{1,0:T(8,128)(2,1)} %tokens.1) | copy-start | bytes 6291460
  7.2 5.9 %copy-start.8 = (bf16[256,512]{1,0:T(8,128)(2,1)S(1)}, bf16[256,512]{1,0:T(8,128)(2,1)}, u32[]{:S(2)}) copy-start(bf16[256,512]{1,0:T(8,128)(2,1)} %param.8) | copy-start | bytes 786436
  7.2 197.6 %all-gather.2.cloned.1.call-start = ((), (), s32[]{:S(2)}) async-start(), calls=%async_computation.1 | async-start | bytes 1179648 | tf_op jit(solution)/shard_map/all_gather | solution.py:305
  10.1 3.4 %copy-start.5 = (bf16[4096,128]{1,0:T(8,128)(2,1)S(1)}, bf16[4096,128]{1,0:T(8,128)(2,1)}, u32[]{:S(2)}) copy-start(bf16[4096,128]{1,0:T(8,128)(2,1)} %weight.1) | copy-start | bytes 3145732
  185.6 3.3 %copy-start.1 = (bf16[8,64,4096]{2,1,0:T(8,128)(2,1)}, bf16[8,64,4096]{2,1,0:T(8,128)(2,1)S(1)}, u32[]{:S(2)}) copy-start(bf16[8,64,4096]{2,1,0:T(8,128)(2,1)S(1)} %get-tuple-element.7) | copy-start | bytes 12582916
  185.6 3.3 %copy-start.3 = (bf16[8,64,512]{2,1,0:T(8,128)(2,1)}, bf16[8,64,512]{2,1,0:T(8,128)(2,1)S(1)}, u32[]{:S(2)}) copy-start(bf16[8,64,512]{2,1,0:T(8,128)(2,1)S(1)} %get-tuple-element.8) | copy-start | bytes 1572868
  185.6 3.3 %copy-start.6 = (f32[256,512]{1,0:T(8,128)}, f32[256,512]{1,0:T(8,128)S(1)}, u32[]{:S(2)}) copy-start(f32[256,512]{1,0:T(8,128)S(1)} %get-tuple-element.6) | copy-start | bytes 1572868
  185.6 2.9 %copy-start.9 = (bf16[2,64,512]{2,1,0:T(8,128)(2,1)S(1)}, bf16[2,64,512]{2,1,0:T(8,128)(2,1)}, u32[]{:S(2)}) copy-start(bf16[2,64,512]{2,1,0:T(8,128)(2,1)} %param.11) | copy-start | bytes 393220
  186.9 2.8 %collective-permute-start = (f32[8,2,32,64]{3,2,0,1:T(8,128)S(1)}, f32[8,2,32,64]{3,2,0,1:T(8,128)S(1)}, u32[]{:S(2)}, u32[]{:S(2)}) collective-permute-start(f32[8,2,32,64]{3,2,0,1:T(8,128)S(1)} %fusion.9), channel_id=1, source_target_pairs={{0,1},{1,0},{2,3},{3,2},{4,5},{5,4},{6,7},{7,6},{8,9},{9,8},{10,11... | collective-permute-start | bytes 393224 | tf_op jit(solution)/shard_map/ppermute | solution.py:275
  188.8 6.4 %collective-permute-start.1 = (f32[8,2,32,64]{3,2,0,1:T(8,128)S(1)}, f32[8,2,32,64]{3,2,0,1:T(8,128)S(1)}, u32[]{:S(2)}, u32[]{:S(2)}) collective-permute-start(f32[8,2,32,64]{3,2,0,1:T(8,128)S(1)} %convolution_bitcast_fusion.3), channel_id=1, source_target_pairs={{0,1},{1,0},{2,3},{3,2},{4,5},{5,4},{6,7},{7,6},{8,9},{9,8},{10,11... | collective-permute-start | bytes 393224 | tf_op jit(solution)/shard_map/ppermute | solution.py:275
  189.0 10.3 %copy-start.4 = (bf16[8,64,512]{2,1,0:T(8,128)(2,1)S(1)}, bf16[8,64,512]{2,1,0:T(8,128)(2,1)}, u32[]{:S(2)}) copy-start(bf16[8,64,512]{2,1,0:T(8,128)(2,1)} %copy-done.3) | copy-start | bytes 1572868
  189.8 15.1 %copy-start.7 = (f32[256,512]{1,0:T(8,128)S(1)}, f32[256,512]{1,0:T(8,128)}, u32[]{:S(2)}) copy-start(f32[256,512]{1,0:T(8,128)} %copy-done.6) | copy-start | bytes 1572868
  190.6 12.1 %all-to-all-start = ((f32[8,1,4096]{2,1,0:T(1,128)}), f32[8,1,4096]{2,1,0:T(1,128)S(1)}, u32[]{:S(2)}, u32[]{:S(2)}) async-start(f32[8,1,4096]{2,1,0:T(1,128)} %reshape.149), calls=%async_computation | async-start | bytes 262144 | tf_op jit(solution)/shard_map/all_to_all | solution.py:320
Sparse Core Ops, SparseCore 0:
  10.2 111.5 all-gather.1

commit v2 on v1

--- a/solution.py
+++ b/solution.py
@@ -86,10 +86,12 @@
 
 
 def exchange_kernel(
-    weight, tokens, sent_tok, sent_grad,
-    base, got_tok, got_grad,
+    weight, tokens, sent_tok, sent_grad, down, up,
+    base, down_grad, up_grad, home,
     blocks, tok, acc, keep_own, keep_far, from_core, from_group,
+    got_tok, got_grad, part, far_part, low, landed,
     up_s, up_r, down_s, down_r, side_s, side_r, local, tok_s, tok_r, grad_s, grad_r, one_s, one_r,
+    core_s, core_r, back_s, back_r,
 ):
     group = lax.axis_index("groups")
     me = lax.axis_index("wide")
@@ -141,20 +143,22 @@
     for copy in own:
         copy.start()
 
-    routed = []
-    for k in range(1, 8):
-        for src, dst, send, recv in (
-            (sent_grad, got_grad, grad_s, grad_r), (sent_tok, got_tok, tok_s, tok_r)
-        ):
-            copy = pltpu.make_async_remote_copy(
-                src_ref=src.at[me ^ k], dst_ref=dst.at[me],
-                send_sem=send.at[k], recv_sem=recv.at[k],
-                device_id={"wide": me ^ k}, device_id_type=MESH,
-            )
-            copy.start()
-            routed.append(copy)
-
-    for d in range(1, 4):
+    def route(src, dst, send, recv, k):
+        return pltpu.make_async_remote_copy(
+            src_ref=src.at[me ^ k], dst_ref=dst.at[me],
+            send_sem=send.at[k], recv_sem=recv.at[k],
+            device_id={"wide": me ^ k}, device_id_type=MESH,
+        )
+
+    toks, grads = {}, {}
+    for k in (1, 2, 3, 4, 5, 6, 7):
+        grads[k] = route(sent_grad, got_grad, grad_s, grad_r, k)
+        grads[k].start()
+    for k in (1, 2, 3):
+        toks[k] = route(sent_tok, got_tok, tok_s, tok_r, k)
+        toks[k].start()
+
+    for d in range(1, 3):
         for c in range(PIECES):
             @pl.when(z >= d)
             def _():
@@ -179,6 +183,37 @@
                     step(False, slot, c, me - 2, down_s.at[at, c], down_r.at[at, c]).start()
 
                 step(False, slot, c, me ^ 1, side_s.at[at, c], side_r.at[at, c]).start()
+
+    for k in (4, 5, 6, 7):
+        toks[k] = route(sent_tok, got_tok, tok_s, tok_r, k)
+        toks[k].start()
+
+    for d in range(3, 4):
+        for c in range(PIECES):
+            @pl.when(z >= d)
+            def _():
+                at = z - d
+                slot = 2 * at + x
+                step(False, slot, c, me ^ 1, up_s.at[at, c], up_r.at[at, c]).wait_recv()
+
+                @pl.when(z < 3)
+                def _():
+                    step(False, slot, c, me + 2, up_s.at[at, c], up_r.at[at, c]).start()
+
+                step(False, slot, c, me ^ 1, side_s.at[at, c], side_r.at[at, c]).start()
+
+            @pl.when(z + d < 4)
+            def _():
+                at = z + d
+                slot = 2 * at + x
+                step(False, slot, c, me ^ 1, down_s.at[at, c], down_r.at[at, c]).wait_recv()
+
+                @pl.when(z > 0)
+                def _():
+                    step(False, slot, c, me - 2, down_s.at[at, c], down_r.at[at, c]).start()
+
+                step(False, slot, c, me ^ 1, side_s.at[at, c], side_r.at[at, c]).start()
+
 
     for at in range(4):
         for c in range(PIECES):
@@ -228,27 +263,98 @@
             @pl.when((at >= z) & (z > 0))
             def _():
                 step(False, 2 * at + x, c, me ^ 1, down_s.at[at, c], down_r.at[at, c]).wait_send()
-    own[2].wait()
-    own[3].wait()
-    for copy in routed:
-        copy.wait()
-
-
-def exchange(weight, tokens, sent_tok, sent_grad):
+    slots = got_tok.shape[1]
+    width = part.shape[3]
+    row = lax.broadcasted_iota(jnp.int32, (slots, width), 0) // (slots // 2)
+    column_half = lax.broadcasted_iota(jnp.int32, (slots, width), 1) // (width // 2)
+    matches = row == column_half
+    by_row = (((1,), (1,)), ((), ()))
+    shares = []
+    for k in range(8):
+        if k == 0:
+            own[2].wait()
+            own[3].wait()
+        else:
+            grads[k].wait_recv()
+            toks[k].wait_recv()
+        at = me ^ k
+        part[at, 0] = lax.dot_general(
+            got_tok[at], down[...], by_row, preferred_element_type=jnp.float32)
+        part[at, 1] = lax.dot_general(
+            got_grad[at], up[...], by_row, preferred_element_type=jnp.float32)
+        share = pltpu.make_async_remote_copy(
+            src_ref=part.at[at], dst_ref=far_part.at[at],
+            send_sem=core_s.at[k], recv_sem=core_r.at[k],
+            device_id={"narrow": 1 - core}, device_id_type=MESH,
+        )
+        share.start()
+        shares.append(share)
+    backs = []
+    for k in range(8):
+        at = me ^ k
+        shares[k].wait()
+        total_in = jnp.where(matches, part[at, 0] + far_part[at, 0], 0.0)
+        total_out = jnp.where(matches, part[at, 1] + far_part[at, 1], 0.0)
+        low[0, at] = total_in.astype(jnp.bfloat16)
+        low[1, at] = total_out.astype(jnp.bfloat16)
+        if k == 0:
+            home[at] = total_in
+        else:
+            part[at, 0] = total_in
+            back = pltpu.make_async_remote_copy(
+                src_ref=part.at[at, 0], dst_ref=landed.at[me],
+                send_sem=back_s.at[k], recv_sem=back_r.at[k],
+                device_id={"wide": at}, device_id_type=MESH,
+            )
+            back.start()
+            backs.append(back)
+    by_slot = (((0,), (0,)), ((), ()))
+    in_low = low[0].reshape(8 * slots, width)
+    out_low = low[1].reshape(8 * slots, width)
+    tile = up.shape[1]
+
+    def columns(i, carry):
+        at = pl.ds(pl.multiple_of(i * tile, tile), tile)
+        down_grad[:, at] = (
+            adapter_scale
+            * lax.dot_general(
+                out_low, got_tok[:, :, at].reshape(8 * slots, tile), by_slot,
+                preferred_element_type=jnp.float32)
+        ).astype(jnp.bfloat16)
+        return carry
+
+    lax.fori_loop(0, down.shape[1] // tile, columns, 0)
+    up_grad[...] = (
+        adapter_scale
+        * lax.dot_general(
+            in_low, got_grad[...].reshape(8 * slots, tile), by_slot,
+            preferred_element_type=jnp.float32)
+    ).astype(jnp.bfloat16)
+    for k in range(1, 8):
+        backs[k - 1].wait()
+        home[me ^ k] = landed[me ^ k]
+        toks[k].wait_send()
+        grads[k].wait_send()
+
+
+def exchange(weight, tokens, sent_tok, sent_grad, down, up):
     count, width = tokens.shape
     half = width // 2
     out_columns = weight.shape[1] * 4
     anywhere = pl.BlockSpec(memory_space=pl.ANY)
+    vmem = pl.BlockSpec(memory_space=pltpu.VMEM)
     dma = pltpu.SemaphoreType.DMA
+    slots, ranks = sent_tok.shape[1], down.shape[0]
     return pl.pallas_call(
         exchange_kernel,
         out_shape=(
             jax.ShapeDtypeStruct((count, out_columns), jnp.float32),
-            jax.ShapeDtypeStruct(sent_tok.shape, sent_tok.dtype),
-            jax.ShapeDtypeStruct(sent_grad.shape, sent_grad.dtype),
+            jax.ShapeDtypeStruct(down.shape, down.dtype),
+            jax.ShapeDtypeStruct(up.shape, up.dtype),
+            jax.ShapeDtypeStruct((8, slots, ranks), jnp.float32),
         ),
-        in_specs=[anywhere] * 4,
-        out_specs=(pl.BlockSpec(memory_space=pltpu.VMEM), anywhere, anywhere),
+        in_specs=[anywhere] * 4 + [vmem] * 2,
+        out_specs=(vmem,) * 4,
         scratch_shapes=[
             pltpu.VMEM((8, half, 128), jnp.bfloat16),
             pltpu.VMEM((2, count, half), jnp.bfloat16),
@@ -257,22 +363,25 @@
             pltpu.VMEM((4, count, 128), jnp.float32),
             pltpu.VMEM((4, 2 * count, 128), jnp.float32),
             pltpu.VMEM((4, count, 128), jnp.float32),
+            pltpu.VMEM(sent_tok.shape, jnp.bfloat16),
+            pltpu.VMEM(sent_grad.shape, jnp.bfloat16),
+            pltpu.VMEM((8, 2, slots, ranks), jnp.float32),
+            pltpu.VMEM((8, 2, slots, ranks), jnp.float32),
+            pltpu.VMEM((2, 8, slots, ranks), jnp.bfloat16),
+            pltpu.VMEM((8, slots, ranks), jnp.float32),
         ]
         + [dma((4, PIECES))] * 6
         + [dma((4,))]
         + [dma((8,))] * 4
-        + [dma((3,))] * 2,
+        + [dma((3,))] * 2
+        + [dma((8,))] * 4,
         compiler_params=pltpu.CompilerParams(
             collective_id=0, has_side_effects=True, vmem_limit_bytes=40 * 1024 * 1024
         ),
         cost_estimate=pl.CostEstimate(
             flops=2 * 512 * 2048 * 1024, bytes_accessed=40 * 1024 * 1024, transcendentals=0
         ),
-    )(weight, tokens, sent_tok, sent_grad)
-
-
-def over_cores(value):
-    return value + lax.ppermute(value, "narrow", [(0, 1), (1, 0)])
+    )(weight, tokens, sent_tok, sent_grad, down, up)
 
 
 def fused_body(
@@ -303,38 +412,21 @@
     sent_tok = jnp.dot(pick_low, tokens, preferred_element_type=jnp.bfloat16)
     sent_grad = jnp.dot(pick_low, output_gradient, preferred_element_type=jnp.bfloat16)
     all_up = lax.all_gather(adapter_up, "wide", axis=0, tiled=True)
-    base, got_tok, got_grad = exchange(
+    base, down_gradient, up_gradient, home = exchange(
         value_weight,
         tokens,
         sent_tok.reshape(wide_count, resident * per_adapter, -1),
         sent_grad.reshape(wide_count, resident * per_adapter, -1),
-    )
-    got_tok = got_tok.reshape(wide_count, resident, per_adapter, -1)
-    got_grad = got_grad.reshape(wide_count, resident, per_adapter, -1)
-    rank_in = over_cores(
-        jnp.einsum("qopn,onx->qopx", got_tok, adapter_down, preferred_element_type=jnp.float32)
-    )
-    rank_out = over_cores(
-        jnp.einsum("gzme,zte->gzmt", got_grad, adapter_up, preferred_element_type=jnp.float32)
-    )
-    home = lax.all_to_all(rank_in, "wide", split_axis=0, concat_axis=0, tiled=True)
-    in_low = rank_in.astype(jnp.bfloat16)
-    out_low = rank_out.astype(jnp.bfloat16)
-    down_gradient = (
-        adapter_scale
-        * jnp.einsum("wjkd,wjkr->jdr", got_tok, out_low, preferred_element_type=jnp.float32)
-    ).astype(jnp.bfloat16)
-    up_gradient = (
-        adapter_scale
-        * jnp.einsum("wjkr,wjkc->jrc", in_low, got_grad, preferred_element_type=jnp.float32)
-    ).astype(jnp.bfloat16)
+        jnp.swapaxes(adapter_down, 1, 2).reshape(resident * rank, -1),
+        adapter_up.reshape(resident * rank, -1),
+    )
+    down_gradient = jnp.swapaxes(down_gradient.reshape(resident, rank, -1), 1, 2)
+    up_gradient = up_gradient.reshape(adapter_up.shape)
     ranks = lax.dot_general(
-        pick.astype(jnp.float32), home.reshape(adapters * per_adapter, rank),
+        pick.astype(jnp.float32), home.reshape(adapters * per_adapter, resident * rank),
         (((0,), (0,)), ((), ())), precision=exact,
     )
-    owner = (position[:, None] >= slot_starts[None, :]) & (
-        position[:, None] < (slot_starts + slot_counts)[None, :]
-    )
+    owner = jnp.any(pick.reshape(wide_count, resident * per_adapter, tok_rows), axis=1).T
     spread = jnp.where(owner[:, :, None], ranks[:, None, :], 0.0)
     lora = jnp.dot(
         spread.reshape(tok_rows, adapters * rank),

time: 215 us -> 180 us (0.84)
  Pallas kernels: 172 us -> 153 us
  starting transfers between devices: 6.4 us -> 0.04 us
  matrix products: 13.2 us -> 7.02 us
  waiting for transfers between devices: 3.78 us -> 0.7 us
    pallas_call x1, Pallas kernels: 172 us -> 153 us  [exchange(): pl.pallas_call(exchange_kernel, out_shape=(jax.ShapeDtypeStruct((count, o...]
    dot_general x4 -> x0, matrix products: 6.45 us -> none  [the longest x1 4.05 us: fused_body(): jnp.einsum('wjkd,wjkr->jdr', got_tok, out_low, preferred_element_type=jnp...]
    all_to_all x1 -> x0, starting transfers between devices: 4.63 us -> none  [fused_body(): lax.all_to_all(rank_in, 'wide', split_axis=0, concat_axis=0, tiled=True)]
    all_to_all x1 -> x0, waiting for transfers between devices: 2.54 us -> none  [fused_body(): lax.all_to_all(rank_in, 'wide', split_axis=0, concat_axis=0, tiled=True)]
  transfers between devices with their start and end apart: 4 -> 1, of which waited for: 2 -> 0; matrix products, arithmetic and copies ran while one was open for 7% -> 4% of each run, Pallas kernels for 80% -> 85%
where the time goes in v2:
time: 180 us; the launch traced here: 179 us
  Pallas kernels  153 us (85%)
  between operations  14.2 us (8%)
  matrix products  7.02 us (4%)
  local copies, waits for them, and re-layouts  2.47 us (1%)
  other arithmetic  2.15 us (1%)
    pallas_call x1, Pallas kernels, exchange(): pl.pallas_call(exchange_kernel, out_shape=(jax.ShapeDtypeStruct((count, o...  153 us
  transfers between devices with their start and end apart: 1, of which 0 were waited for; matrix products, arithmetic and copies ran while one was open for 4% of the time, Pallas kernels for 85%

profile of v2, /device:TPU:0, one launch (start us, length us, event | category | flops | bytes accessed | tf_op | source)
XLA Modules:
  0.0 179.5 jit_solution(7176886801954800921)
XLA Ops:
  7.2 0.0 copy-start
  7.2 0.0 all-gather.2.cloned.1.call-start
  7.2 0.7 all-gather.2.cloned.1.call-update
  7.9 0.8 select_reduce_fusion.1
  8.7 0.8 select_reduce_fusion.2
  9.5 0.1 add.28
  9.6 0.1 add.29
  9.6 0.1 add.30
  9.7 0.1 lt.55
  9.8 0.1 lt.56
  9.9 0.1 lt.57
  10.0 0.1 lt.53
  10.0 0.1 add_select_fusion
  10.1 0.1 select_n.30
  10.2 0.2 fusion.6
  10.4 0.2 copy.13
  10.5 0.0 copy-done
  10.6 0.3 fusion.7.sent_grad
  10.9 0.0 copy-start.1
  10.9 0.0 copy-start.2
  10.9 0.0 copy-start.3
  10.9 0.0 copy-start.4
  11.0 3.0 %fusion.sent_tok = bf16[8,64,4096]{2,1,0:T(8,128)(2,1)S(1)} fusion(bf16[256,4096]{1,0:T(8,128)(2,1)} %tokens.1, s32[8,64]{1,0:T(8,128)S(1)} %add_select_fusion.1), kind=kOutput, calls=%fused_computation | convolution fusion | flops 1073872896 | bytes 6293504 | tf_op jit(solution)/shard_map/dot_general | solution.py:412
  14.0 0.0 copy-done.1
  14.0 0.0 copy-done.2
  14.0 0.0 copy-done.3
  14.0 0.0 copy-done.4
  14.0 153.0 %shard_map.94 = (f32[256,512]{1,0:T(8,128)S(1)}, bf16[128,4096]{1,0:T(8,128)(2,1)S(1)}, bf16[128,512]{1,0:T(8,128)(2,1)S(1)}, f32[8,64,128]{2,1,0:T(8,128)S(1)}) custom-call(bf16[4096,128]{1,0:T(8,128)(2,1)S(1)} %copy-done.2, bf16[256,4096]{1,0:T(8,128)(2,1)S(1)} %copy-done.1, bf16[8,64,4096]{2,1,0:T(8,128)(2,1)S(1)} %fusion.sent_tok, ...), custom_call_target="tpu_custom_call" | custom-call | flops 2147483648 | bytes 41943040 | tf_op jit(solution)/shard_map/pallas_call | solution.py:348
  167.0 0.7 fusion.8
  167.7 0.3 broadcast_select_fusion
  168.0 0.0 all-gather.2.cloned.1.call-done
  168.1 3.0 %fusion.3 = bf16[256,512]{1,0:T(8,128)(2,1)} fusion(f32[256,512]{1,0:T(8,128)S(1)} %get-tuple-element.7, bf16[1024,512]{1,0:T(8,128)(2,1)} %bitcast.30, f32[32,8,8,128]{3,2,1,0:T(8,128)S(1)} %bitcast.29), kind=kOutput, calls=%fused_computation.4 | convolution fusion | flops 1611005952 | bytes 2883584 | tf_op jit(solution)/shard_map/dot_general | solution.py:431
  171.0 1.0 copy.21
  172.0 0.7 copy.22
  (2 shorter events, 0.0 us)
Async XLA Ops:
  7.2 3.4 %copy-start = (bf16[256,512]{1,0:T(8,128)(2,1)S(1)}, bf16[256,512]{1,0:T(8,128)(2,1)}, u32[]{:S(2)}) copy-start(bf16[256,512]{1,0:T(8,128)(2,1)} %param.8) | copy-start | bytes 786436
  7.2 160.9 %all-gather.2.cloned.1.call-start = ((), (), s32[]{:S(2)}) async-start(), calls=%async_computation | async-start | bytes 1179648 | tf_op jit(solution)/shard_map/all_gather | solution.py:414
  10.9 3.1 %copy-start.1 = (bf16[256,4096]{1,0:T(8,128)(2,1)S(1)}, bf16[256,4096]{1,0:T(8,128)(2,1)}, u32[]{:S(2)}) copy-start(bf16[256,4096]{1,0:T(8,128)(2,1)} %tokens.1) | copy-start | bytes 6291460
  10.9 3.1 %copy-start.2 = (bf16[4096,128]{1,0:T(8,128)(2,1)S(1)}, bf16[4096,128]{1,0:T(8,128)(2,1)}, u32[]{:S(2)}) copy-start(bf16[4096,128]{1,0:T(8,128)(2,1)} %weight.1) | copy-start | bytes 3145732
  10.9 3.1 %copy-start.3 = (bf16[2,4096,64]{1,2,0:T(8,128)(2,1)S(1)}, bf16[2,4096,64]{1,2,0:T(8,128)(2,1)}, u32[]{:S(2)}) copy-start(bf16[2,4096,64]{1,2,0:T(8,128)(2,1)} %param.10) | copy-start | bytes 3145732
  10.9 3.1 %copy-start.4 = (bf16[2,64,512]{2,1,0:T(8,128)(2,1)S(1)}, bf16[2,64,512]{2,1,0:T(8,128)(2,1)}, u32[]{:S(2)}) copy-start(bf16[2,64,512]{2,1,0:T(8,128)(2,1)} %param.11) | copy-start | bytes 393220
Sparse Core Ops, SparseCore 0:
  10.1 52.5 all-gather.1

commit v3 on v2

--- a/solution.py
+++ b/solution.py
@@ -6,7 +6,7 @@
 from jax.sharding import PartitionSpec as P
 
 MESH = pl.DeviceIdType.MESH
-PIECES = 4
+PIECES = 2
 
 adapter_scale = 2.0
 
@@ -151,42 +151,42 @@
         )
 
     toks, grads = {}, {}
+    for k in (1, 2, 3):
+        toks[k] = route(sent_tok, got_tok, tok_s, tok_r, k)
+        toks[k].start()
+
+    for d in range(1, 3):
+        for c in range(PIECES):
+            @pl.when(z >= d)
+            def _():
+                at = z - d
+                slot = 2 * at + x
+                step(False, slot, c, me ^ 1, up_s.at[at, c], up_r.at[at, c]).wait_recv()
+
+                @pl.when(z < 3)
+                def _():
+                    step(False, slot, c, me + 2, up_s.at[at, c], up_r.at[at, c]).start()
+
+                step(False, slot, c, me ^ 1, side_s.at[at, c], side_r.at[at, c]).start()
+
+            @pl.when(z + d < 4)
+            def _():
+                at = z + d
+                slot = 2 * at + x
+                step(False, slot, c, me ^ 1, down_s.at[at, c], down_r.at[at, c]).wait_recv()
+
+                @pl.when(z > 0)
+                def _():
+                    step(False, slot, c, me - 2, down_s.at[at, c], down_r.at[at, c]).start()
+
+                step(False, slot, c, me ^ 1, side_s.at[at, c], side_r.at[at, c]).start()
+
+    for k in (4, 5, 6, 7):
+        toks[k] = route(sent_tok, got_tok, tok_s, tok_r, k)
+        toks[k].start()
     for k in (1, 2, 3, 4, 5, 6, 7):
         grads[k] = route(sent_grad, got_grad, grad_s, grad_r, k)
         grads[k].start()
-    for k in (1, 2, 3):
-        toks[k] = route(sent_tok, got_tok, tok_s, tok_r, k)
-        toks[k].start()
-
-    for d in range(1, 3):
-        for c in range(PIECES):
-            @pl.when(z >= d)
-            def _():
-                at = z - d
-                slot = 2 * at + x
-                step(False, slot, c, me ^ 1, up_s.at[at, c], up_r.at[at, c]).wait_recv()
-
-                @pl.when(z < 3)
-                def _():
-                    step(False, slot, c, me + 2, up_s.at[at, c], up_r.at[at, c]).start()
-
-                step(False, slot, c, me ^ 1, side_s.at[at, c], side_r.at[at, c]).start()
-
-            @pl.when(z + d < 4)
-            def _():
-                at = z + d
-                slot = 2 * at + x
-                step(False, slot, c, me ^ 1, down_s.at[at, c], down_r.at[at, c]).wait_recv()
-
-                @pl.when(z > 0)
-                def _():
-                    step(False, slot, c, me - 2, down_s.at[at, c], down_r.at[at, c]).start()
-
-                step(False, slot, c, me ^ 1, side_s.at[at, c], side_r.at[at, c]).start()
-
-    for k in (4, 5, 6, 7):
-        toks[k] = route(sent_tok, got_tok, tok_s, tok_r, k)
-        toks[k].start()
 
     for d in range(3, 4):
         for c in range(PIECES):

time: 180 us -> 179 us (level)
  no operation moved by 1% of the time
where the time goes in v3:
time: 179 us
  Pallas kernels  152 us (85%)
  between operations  14.2 us (8%)
  matrix products  7.02 us (4%)
  local copies, waits for them, and re-layouts  2.47 us (1%)
  other arithmetic  2.15 us (1%)
    pallas_call x1, Pallas kernels, exchange(): pl.pallas_call(exchange_kernel, out_shape=(jax.ShapeDtypeStruct((count, o...  152 us
  transfers between devices with their start and end apart: 1, of which 0 were waited for; matrix products, arithmetic and copies ran while one was open for 4% of the time, Pallas kernels for 85%

profile of v3, /device:TPU:0, one launch (start us, length us, event | category | flops | bytes accessed | tf_op | source)
XLA Modules:
  0.0 178.9 jit_solution(8103285555213996884)
XLA Ops:
  7.2 0.0 copy-start
  7.2 0.0 all-gather.2.cloned.1.call-start
  7.2 0.7 all-gather.2.cloned.1.call-update
  7.9 0.8 select_reduce_fusion.1
  8.7 0.8 select_reduce_fusion.2
  9.5 0.1 add.28
  9.6 0.1 add.29
  9.6 0.1 add.30
  9.7 0.1 lt.55
  9.8 0.1 lt.56
  9.9 0.1 lt.57
  10.0 0.1 lt.53
  10.0 0.1 add_select_fusion
  10.1 0.1 select_n.30
  10.2 0.2 fusion.6
  10.4 0.2 copy.13
  10.5 0.0 copy-done
  10.6 0.3 fusion.7.sent_grad
  10.9 0.0 copy-start.1
  10.9 0.0 copy-start.2
  10.9 0.0 copy-start.3
  10.9 0.0 copy-start.4
  11.0 3.0 %fusion.sent_tok = bf16[8,64,4096]{2,1,0:T(8,128)(2,1)S(1)} fusion(bf16[256,4096]{1,0:T(8,128)(2,1)} %tokens.1, s32[8,64]{1,0:T(8,128)S(1)} %add_select_fusion.1), kind=kOutput, calls=%fused_computation | convolution fusion | flops 1073872896 | bytes 6293504 | tf_op jit(solution)/shard_map/dot_general | solution.py:412
  14.0 0.0 copy-done.1
  14.0 0.0 copy-done.2
  14.0 0.0 copy-done.3
  14.0 0.0 copy-done.4
  14.0 152.4 %shard_map.94 = (f32[256,512]{1,0:T(8,128)S(1)}, bf16[128,4096]{1,0:T(8,128)(2,1)S(1)}, bf16[128,512]{1,0:T(8,128)(2,1)S(1)}, f32[8,64,128]{2,1,0:T(8,128)S(1)}) custom-call(bf16[4096,128]{1,0:T(8,128)(2,1)S(1)} %copy-done.2, bf16[256,4096]{1,0:T(8,128)(2,1)S(1)} %copy-done.1, bf16[8,64,4096]{2,1,0:T(8,128)(2,1)S(1)} %fusion.sent_tok, ...), custom_call_target="tpu_custom_call" | custom-call | flops 2147483648 | bytes 41943040 | tf_op jit(solution)/shard_map/pallas_call | solution.py:348
  166.4 0.7 fusion.8
  167.1 0.3 broadcast_select_fusion
  167.4 0.0 all-gather.2.cloned.1.call-done
  167.5 3.0 %fusion.3 = bf16[256,512]{1,0:T(8,128)(2,1)} fusion(f32[256,512]{1,0:T(8,128)S(1)} %get-tuple-element.7, bf16[1024,512]{1,0:T(8,128)(2,1)} %bitcast.30, f32[32,8,8,128]{3,2,1,0:T(8,128)S(1)} %bitcast.29), kind=kOutput, calls=%fused_computation.4 | convolution fusion | flops 1611005952 | bytes 2883584 | tf_op jit(solution)/shard_map/dot_general | solution.py:431
  170.4 1.0 copy.21
  171.4 0.7 copy.22
  (2 shorter events, 0.0 us)
Async XLA Ops:
  7.2 3.4 %copy-start = (bf16[256,512]{1,0:T(8,128)(2,1)S(1)}, bf16[256,512]{1,0:T(8,128)(2,1)}, u32[]{:S(2)}) copy-start(bf16[256,512]{1,0:T(8,128)(2,1)} %param.8) | copy-start | bytes 786436
  7.2 160.3 %all-gather.2.cloned.1.call-start = ((), (), s32[]{:S(2)}) async-start(), calls=%async_computation | async-start | bytes 1179648 | tf_op jit(solution)/shard_map/all_gather | solution.py:414
  10.9 3.1 %copy-start.1 = (bf16[256,4096]{1,0:T(8,128)(2,1)S(1)}, bf16[256,4096]{1,0:T(8,128)(2,1)}, u32[]{:S(2)}) copy-start(bf16[256,4096]{1,0:T(8,128)(2,1)} %tokens.1) | copy-start | bytes 6291460
  10.9 3.1 %copy-start.2 = (bf16[4096,128]{1,0:T(8,128)(2,1)S(1)}, bf16[4096,128]{1,0:T(8,128)(2,1)}, u32[]{:S(2)}) copy-start(bf16[4096,128]{1,0:T(8,128)(2,1)} %weight.1) | copy-start | bytes 3145732
  10.9 3.1 %copy-start.3 = (bf16[2,4096,64]{1,2,0:T(8,128)(2,1)S(1)}, bf16[2,4096,64]{1,2,0:T(8,128)(2,1)}, u32[]{:S(2)}) copy-start(bf16[2,4096,64]{1,2,0:T(8,128)(2,1)} %param.10) | copy-start | bytes 3145732
  10.9 3.1 %copy-start.4 = (bf16[2,64,512]{2,1,0:T(8,128)(2,1)S(1)}, bf16[2,64,512]{2,1,0:T(8,128)(2,1)}, u32[]{:S(2)}) copy-start(bf16[2,64,512]{2,1,0:T(8,128)(2,1)} %param.11) | copy-start | bytes 393220
Sparse Core Ops, SparseCore 0:
  10.1 71.7 all-gather.1
